TPU v7x, 32 devices: a whole 2x2x4 slice. The times are simulated.
32 devices in a mesh: rows: 8 (over z, x), head: 4 (over y, core).
Axes of the slice: x: 2, y: 2, z: 4, core: 2. Of those that a mesh axis runs over, the one named last changes fastest.
Arguments:
- media: bfloat16 [32, 256, 1536], P('rows', 'head'), may hold values from -6 to 6
- latents: bfloat16 [32, 64, 1536], P('rows', 'head'), may hold values from -6 to 6
- counts: int32 [4], replicated, may hold values from 1 to 8, 20 in all
- media_gain: float32 [1536], replicated, may hold values from 0.1 to 1.9
- media_shift: float32 [1536], replicated, may hold values from -1.5 to 1.5
- latent_gain: float32 [1536], replicated, may hold values from 0.1 to 1.9
- latent_shift: float32 [1536], replicated, may hold values from -1.5 to 1.5
- w_query: bfloat16 [1536, 1536], replicated, may hold values from -0.15625 to 0.15625
- w_key: bfloat16 [1536, 1536], replicated, may hold values from -0.15625 to 0.15625
- w_value: bfloat16 [1536, 1536], replicated, may hold values from -0.15625 to 0.15625
- w_out: bfloat16 [1536, 1536], replicated, may hold values from -1.25 to 1.25
- ffn_gain: float32 [1536], replicated, may hold values from 0.1 to 1.9
- ffn_shift: float32 [1536], replicated, may hold values from -1.5 to 1.5
- w_up: bfloat16 [1536, 6144], replicated, may hold values from -0.15625 to 0.15625
- w_down: bfloat16 [6144, 1536], replicated, may hold values from -0.078125 to 0.078125
- cotangent: bfloat16 [32, 64, 1536], P('rows', 'head'), may hold values from -6 to 6
Outputs:
- latents_out: float32 [32, 64, 1536], P('rows', 'head')
- media_grad: float32 [32, 256, 1536], P('rows', 'head')
- latents_grad: float32 [32, 64, 1536], P('rows', 'head')
- media_gain_grad: float32 [1536], P(('rows', 'head'))
- media_shift_grad: float32 [1536], P(('rows', 'head'))
- latent_gain_grad: float32 [1536], P(('rows', 'head'))
- latent_shift_grad: float32 [1536], P(('rows', 'head'))
- query_grad: float32 [1536, 1536], P('rows', 'head')
- key_grad: float32 [1536, 1536], P('rows', 'head')
- value_grad: float32 [1536, 1536], P('rows', 'head')
- out_grad: float32 [1536, 1536], P('rows', 'head')
- ffn_gain_grad: float32 [1536], P(('rows', 'head'))
- ffn_shift_grad: float32 [1536], P(('rows', 'head'))
- up_grad: float32 [1536, 6144], P('rows', 'head')
- down_grad: float32 [6144, 1536], P('head', 'rows')
Inputs may be any that keep to these rules, and one draw needn't show every extreme that they name: At most 8 images in a sequence, and some sequence has exactly 8; the counts sum to 20.
All inputs are finite; a program needn't handle non-finite values.
Results may differ from a plain program's by a relative error of at most 0.017.
Values may be sent and summed in bfloat16 or wider, within the bound.
A program may use at most 192 MiB of HBM per device.

v0:
```python
import functools
import math
import types

import jax
import jax.numpy as jnp
from jax import lax
from jax.experimental import pallas as pl
from jax.experimental.pallas import tpu as pltpu
from jax.sharding import PartitionSpec as P

HEAD_DIM = 96
MAX_IMG = 8
EPSILON = 1e-05
BF = jnp.bfloat16
F32 = jnp.float32
MESH = pl.DeviceIdType.MESH
ANY = pl.BlockSpec(memory_space=pl.ANY)
VMEM = pl.BlockSpec(memory_space=pltpu.VMEM)
SMEM = pl.BlockSpec(memory_space=pltpu.SMEM)


def factor_rows(count):
    nz = 4 if count % 4 == 0 else 1
    return nz, count // nz


def factor_head(count):
    nc = 2 if count % 2 == 0 else 1
    return count // nc, nc


def mm(a, b):
    return lax.dot_general(a, b, (((1,), (0,)), ((), ())), preferred_element_type=F32)


def mt(a, b):
    return lax.dot_general(a, b, (((1,), (1,)), ((), ())), preferred_element_type=F32)


def tm(a, b):
    return lax.dot_general(a, b, (((0,), (0,)), ((), ())), preferred_element_type=F32)


class Place:
    def __init__(self, rows, heads):
        self.rows, self.heads = rows, heads
        self.nz, self.nx = factor_rows(rows)
        self.ny, self.nc = factor_head(heads)
        self.r = lax.axis_index("rows")
        self.h = lax.axis_index("head")
        self.z, self.x = self.r // self.nx, self.r % self.nx
        self.y, self.c = self.h // self.nc, self.h % self.nc

    def y_peer(self, d):
        return lax.rem(self.y + d, self.ny)

    def group(self, dz, dx):
        return lax.rem(self.z + dz, self.nz) * self.nx + lax.rem(self.x + dx, self.nx)

    def head_of(self, slot):
        d, e = divmod(slot, self.nc)
        return self.y_peer(d) * self.nc + (self.c if e == 0 else self.nc - 1 - self.c)

    def on_y(self, d):
        return self.r, self.y_peer(d) * self.nc + self.c

    def on_x(self, d):
        return self.group(0, d), self.h

    def on_z(self, d):
        return self.group(d, 0), self.h

    def partner(self):
        return self.r, self.y * self.nc + (self.nc - 1 - self.c)

    def greet(self):
        peers = [(self.r, lax.rem(self.h + d, self.heads)) for d in range(1, self.heads)]
        peers += [self.on_x(d) for d in range(1, self.nx)] + [self.on_z(d) for d in range(1, self.nz)]
        barrier = pltpu.get_barrier_semaphore()
        for peer in peers:
            pl.semaphore_signal(barrier, inc=1, device_id=peer, device_id_type=MESH)
        pl.semaphore_wait(barrier, len(peers))


class Copies:
    def __init__(self, at, send, recv, local):
        self.at, self.send, self.recv, self.local = at, send, recv, local
        self.used, self.used_local = 0, 0
        self.unsent, self.open = [], []

    def plan(self, src, dst, peer):
        copy = pltpu.make_async_remote_copy(
            src_ref=src,
            dst_ref=dst,
            send_sem=self.send.at[self.used],
            recv_sem=self.recv.at[self.used],
            device_id=peer,
            device_id_type=MESH,
        )
        self.used += 1
        self.unsent.append(copy)
        return copy

    def put(self, src, dst, peer):
        copy = self.plan(src, dst, peer)
        copy.start()
        return copy

    def put_y(self, src, dst):
        return [self.put(src, dst, self.at.on_y(d)) for d in range(1, self.at.ny)]

    def put_x(self, src, dst):
        return [self.put(src, dst, self.at.on_x(d)) for d in range(1, self.at.nx)]

    def put_z(self, src, dst):
        return [self.put(src, dst, self.at.on_z(d)) for d in range(1, self.at.nz)]

    def put_core(self, src, dst):
        return [self.put(src, dst, self.at.partner())] if self.at.nc > 1 else []

    def sent(self, copies):
        for copy in copies:
            copy.wait_send()
        self.unsent = [c for c in self.unsent if all(c is not d for d in copies)]

    def plan_move(self, src, dst):
        copy = pltpu.make_async_copy(src, dst, self.local.at[self.used_local])
        self.used_local += 1
        self.open.append(copy)
        return copy

    def move(self, src, dst):
        copy = self.plan_move(src, dst)
        copy.start()
        return copy

    def moved(self, *copies):
        for copy in copies:
            copy.wait()
        self.open = [c for c in self.open if all(c is not d for d in copies)]

    def finish(self):
        for copy in self.unsent:
            copy.wait_send()
        for copy in self.open:
            copy.wait()


def begin(copies):
    for copy in copies:
        copy.start()


def arrived(copies):
    for copy in copies:
        copy.wait_recv()


def norm_rows(block):
    mean = jnp.mean(block, axis=-1, keepdims=True)
    centered = block - mean
    scale = lax.rsqrt(jnp.mean(centered * centered, axis=-1, keepdims=True) + EPSILON)
    return centered * scale, scale


def sweep(first, last, step, carry=0):
    together = next(k for k in (4, 2, 1) if (last - first) // 16 % k == 0)

    def turn(i, value):
        for j in range(together):
            start = first + i * (16 * together) + j * 16
            value = step(pl.ds(pl.multiple_of(start, 16), 16), value)
        return value

    return lax.fori_loop(0, (last - first) // (16 * together), turn, carry)


def gelu_pair(v):
    c = math.sqrt(2.0 / math.pi)
    square = v * v
    t = jnp.tanh(c * v * (1.0 + 0.044715 * square))
    half = 0.5 * (1.0 + t)
    slope = half + 0.5 * v * (1.0 - t * t) * (c * (1.0 + 3.0 * 0.044715 * square))
    return v * half, slope


def softmax(scores):
    powers = jnp.exp(scores - jnp.max(scores, axis=-1, keepdims=True))
    return powers * (1.0 / jnp.sum(powers, axis=-1, keepdims=True))


def head_mask(heads_here, rows, cols):
    shape = (heads_here * rows, cols)
    row = lax.broadcasted_iota(jnp.int32, shape, 0) // rows
    col = lax.broadcasted_iota(jnp.int32, shape, 1) // HEAD_DIM
    return (row == col).astype(F32)


def spread_heads(block, mask):
    return jnp.concatenate([block] * (mask.shape[0] // block.shape[0]), axis=0) * mask


def gather_heads(block, mask, rows):
    block = block * mask
    return sum(block[j * rows : (j + 1) * rows] for j in range(block.shape[0] // rows))


def sizes_of(s):
    ny, nc = factor_head(s.heads)
    nz, nx = factor_rows(s.rows)
    t = types.SimpleNamespace(ny=ny, nc=nc, nz=nz, nx=nx, G=s.images, D=s.width, E=s.cols, F=s.mine, H=s.heads)
    t.pr, t.ll = s.patch, s.lat
    t.M, t.L, t.LR = t.G * t.pr, t.G * t.ll, t.H * t.ll
    t.GL, t.ML, t.KC = t.G * t.LR, t.M + t.L, t.H * t.pr + t.LR
    t.B = t.D // s.rows
    t.heads_here = t.E // HEAD_DIM
    t.aligned = t.E % 128 == 0
    t.EP = -(-t.E // 128) * 128
    return t


def forward_kernel(s, names, *refs):
    n = types.SimpleNamespace(**dict(zip(names, refs, strict=True)))
    at = Place(s.rows, s.heads)
    t = sizes_of(s)
    ny, nc, nz, nx, G, H = t.ny, t.nc, t.nz, t.nx, t.G, t.H
    M, L, LR, GL, ML, D, E, F, ll, pr = t.M, t.L, t.LR, t.GL, t.ML, t.D, t.E, t.F, t.ll, t.pr
    io = Copies(at, n.send, n.recv, n.local)
    here = at.r

    vectors = ("media_gain", "media_shift", "latent_gain", "latent_shift", "ffn_gain", "ffn_shift")
    load_vecs = [io.move(getattr(n, k), n.vecs.at[i]) for i, k in enumerate(vectors)]
    load_lat = io.move(n.lat, n.raw_l.at[0:L])
    load_cot = io.move(n.cot, n.cot_v)
    load_media = io.move(n.media, n.raw_m.at[0])

    def columns(weight):
        return weight.at[:, pl.ds(pl.multiple_of(at.h * E, 128), E)] if t.aligned else weight

    load_qkv = [io.move(columns(w), v) for w, v in ((n.wk, n.wk_v), (n.wv, n.wv_v), (n.wq, n.wq_v))]
    at.greet()

    chunks = 2
    part = M // chunks

    def far_slot(d):
        return (ny - d) % ny * nc

    def lat_rows(k):
        return n.raw_l.at[k * L : (k + 1) * L]

    lat_far = [io.put(n.lat, lat_rows(far_slot(d)), at.on_y(d)) for d in range(1, ny)]
    lat_near = io.put_core(n.lat, lat_rows(1 % H))
    media_far, media_near = [], []
    for j in range(chunks):
        rows = slice(j * part, (j + 1) * part)
        media_far.append([io.put(n.media.at[rows], n.raw_m.at[far_slot(d), rows], at.on_y(d)) for d in range(1, ny)])
        media_near.append(io.put_core(n.media.at[rows], n.raw_m.at[1 % H, rows]))

    io.moved(load_cot)
    for i in range(G):
        image = here * G + i
        limit = n.counts[image // MAX_IMG]
        live = jnp.where(lax.rem(image, MAX_IMG) < limit, 1.0, 0.0).astype(F32)
        rows = slice(i * ll, (i + 1) * ll)
        n.wide_l[rows] = n.cot_v[rows].astype(F32) * live
    n.dslot[at.y, at.c] = n.wide_l[...].astype(BF)
    own_d = n.dslot.at[at.y, at.c]

    def quarter(r, y):
        return r, pl.ds(pl.multiple_of(y * L, 16), L)

    def across(y, block):
        where = n.dall.at[quarter(here, y)]
        return io.put_z(block, where), io.put_x(block, where)

    z_far, x_far = {}, {}
    z_far[0], x_far[0] = across(at.y, own_d)
    load_out = io.move(n.wout, n.wout_v)
    load_up = io.move(n.wup.at[:, pl.ds(pl.multiple_of(at.h * F, 128), F)], n.wup_v)
    load_down = io.move(n.wdown.at[pl.ds(pl.multiple_of(at.h * F, 16), F)], n.wdown_v)

    def forward_x(d):
        for dz, copy in enumerate(z_far[d], 1):
            copy.wait_recv()
            block = n.dall.at[quarter(at.group(nz - dz, 0), at.y_peer(d))]
            x_far[d] += io.put_x(block, block)

    norm_busy = {}
    turn_count = [0]

    def patches(k, first, last):
        buf = turn_count[0] % 2
        turn_count[0] += 1
        if buf in norm_busy:
            io.moved(norm_busy[buf])

        def step(rows, carry):
            hat, _ = norm_rows(n.raw_m[k, rows].astype(F32))
            n.norm[buf, rows] = (hat * n.vecs[0:1] + n.vecs[1:2]).astype(BF)
            return carry

        sweep(first * 16, last * 16, step)
        rows = slice(first * 16, last * 16)
        for weight, result in ((n.wk_v, n.keys), (n.wv_v, n.values)):
            wide = mm(n.norm[buf, rows], weight[...]).astype(BF)
            for i in range(first * 16 // pr, last * 16 // pr):
                base = i * pr - first * 16
                result[i, k * pr : (k + 1) * pr] = wide[base : base + pr]
        norm_busy[buf] = io.move(n.norm.at[buf, rows], n.key_norm_o.at[k * ML + first * 16 : k * ML + last * 16])

    io.moved(load_media, *load_qkv, *load_vecs)
    patches(0, 0, M // 16)
    if nc > 1:
        for copies in media_near:
            arrived(copies)
        patches(1, 0, M // 16)
    cot_far = io.put_y(own_d, own_d)
    cot_near = io.put_core(own_d, own_d)
    relay = []
    for d, copy in zip(range(1, ny), lat_far):
        copy.wait_recv()
        k = far_slot(d)
        relay += io.put_core(lat_rows(k), lat_rows(k + 1)) if nc > 1 else []
    io.moved(load_lat)
    arrived(lat_near)
    arrived(relay)
    for k in range(H):
        wide = n.raw_l[k * L : (k + 1) * L].astype(F32)
        for i in range(G):
            n.resid[pl.ds(pl.multiple_of(i * LR + at.head_of(k) * ll, 8), ll)] = wide[i * ll : (i + 1) * ll]

    def latent_step(rows, carry):
        hat, _ = norm_rows(n.raw_l[rows].astype(F32))
        n.lnorm[rows] = (hat * n.vecs[2:3] + n.vecs[3:4]).astype(BF)
        return carry

    sweep(0, H * L, latent_step)
    for k in range(H):
        io.move(n.lnorm.at[k * L : (k + 1) * L], n.key_norm_o.at[k * ML + M : (k + 1) * ML])
    for weight, result in ((n.wq_v, n.query), (n.wk_v, n.keys), (n.wv_v, n.values)):
        wide = mm(n.lnorm[...], weight[...])
        for k in range(H):
            for i in range(G):
                n.turn[pl.ds(pl.multiple_of(i * LR + at.head_of(k) * ll, 8), ll)] = wide[k * L + i * ll : k * L + (i + 1) * ll]
        for i in range(G):
            block = n.turn[i * LR : (i + 1) * LR].astype(BF)
            if result is n.query:
                result[i] = block
            else:
                result[i, H * pr : t.KC] = block
    media_relay = []
    for j in range(chunks):
        relays = []
        rows = slice(j * part, (j + 1) * part)
        for d, copy in zip(range(1, ny), media_far[j]):
            copy.wait_recv()
            k = far_slot(d)
            relays.append(io.put_core(n.raw_m.at[k, rows], n.raw_m.at[k + 1, rows]) if nc > 1 else [])
        for d in range(1, ny):
            patches(far_slot(d), j * part // 16, (j + 1) * part // 16)
        for d in range(1, ny):
            if nc > 1:
                arrived(relays[d - 1])
                patches(far_slot(d) + 1, j * part // 16, (j + 1) * part // 16)
    forward_x(0)
    mask = head_mask(t.heads_here, LR, E)
    mask_low = mask.astype(BF)
    scale = 1.0 / math.sqrt(HEAD_DIM)
    for i in range(G):
        scores = mt(spread_heads(n.query[i], mask_low), n.keys[i]) * scale
        probs = softmax(scores).astype(BF)
        mixed = gather_heads(mm(probs, n.values[i]), mask, LR)
        n.mix[at.h, i * LR : (i + 1) * LR] = mixed.astype(BF)
    mix_far = io.put_y(n.mix.at[at.h], n.mix.at[at.h])
    mix_near = io.put_core(n.mix.at[at.h], n.mix.at[at.h])
    for ref, out in ((n.keys, n.keys_o), (n.values, n.values_o), (n.query, n.query_o)):
        io.move(ref, out)
    io.moved(load_out, load_up, load_down)

    def add_mixed(head):
        n.resid[...] += mm(n.mix[head], n.wout_v[pl.ds(pl.multiple_of(head * E, 16), E)])

    add_mixed(at.h)
    arrived(cot_far)
    cot_relay = []
    for d in range(1, ny):
        block = n.dslot.at[at.y_peer(d), at.c]
        cot_relay += io.put_core(block, block)
        z_far[d], x_far[d] = across(at.y_peer(d), block)
    arrived(mix_near)
    if nc > 1:
        add_mixed(at.head_of(1))
    arrived(cot_near)
    arrived(cot_relay)
    for y in range(ny):
        for c in range(nc):
            wide = n.dslot[y, c].astype(F32)
            for i in range(G):
                n.part[i * LR + (y * nc + c) * ll : i * LR + (y * nc + c + 1) * ll] = wide[i * ll : (i + 1) * ll]
    n.dout[...] = n.part[...].astype(BF)
    io.move(n.dout, n.dout_o)
    mix_relay = []
    for d, copy in zip(range(1, ny), mix_far):
        copy.wait_recv()
        block = n.mix.at[at.head_of(far_slot(d))]
        mix_relay.append(io.put_core(block, block))
    for d in range(1, ny):
        add_mixed(at.head_of(far_slot(d)))
    for d in range(1, ny):
        if nc > 1:
            arrived(mix_relay[d - 1])
            add_mixed(at.head_of(far_slot(d) + 1))
    io.move(n.mix, n.mixed_o)
    gain, shift = n.vecs[4:5], n.vecs[5:6]

    def ffn_step(rows, carry):
        hat, inv = norm_rows(n.resid[rows])
        n.hat[rows] = hat
        n.inv[rows] = jnp.broadcast_to(inv, (16, 128))
        n.ffn[rows] = (hat * n.vecs[4:5] + n.vecs[5:6]).astype(BF)
        return carry

    sweep(0, GL, ffn_step)
    io.move(n.ffn, n.ffn_o)

    def own_rows(ref):
        return jnp.concatenate([ref[pl.ds(pl.multiple_of(i * LR + at.h * ll, 8), ll)] for i in range(G)], axis=0)

    n.fq[...] = (own_rows(n.hat) * gain + shift).astype(BF)
    own_f = n.fall.at[at.z]
    ffn_far = io.put_z(n.fq, own_f)
    io.move(n.fq, own_f)
    value, slope = gelu_pair(mm(n.ffn[...], n.wup_v[...]))
    n.act[...] = value.astype(BF)
    n.dhid[...] = (mt(n.dout[...], n.wdown_v[...]) * slope).astype(BF)
    n.part[...] = mt(n.dhid[...], n.wup_v[...])
    half = GL // nc
    mine = pl.ds(pl.multiple_of(at.c * half, 16), half)
    theirs = pl.ds(pl.multiple_of((nc - 1 - at.c) * half, 16), half)
    swap = io.put_core(n.part.at[theirs], n.c_recv)
    io.move(n.act, n.act_o)
    io.move(n.dhid, n.dhid_o)
    out_part = mm(n.act[...], n.wdown_v[...])
    for i in range(G):
        for head in range(H):
            base = i * LR + head * ll
            n.outp[head % nc, head // nc, i * ll : (i + 1) * ll] = out_part[base : base + ll]
    out_swap = io.put_core(n.outp.at[nc - 1 - at.c], n.oc_recv)
    arrived(swap)
    total = n.part[mine]
    if nc > 1:
        total = total + n.c_recv[...]
    n.y_send[...] = total.astype(BF)
    sum_far = [io.put(n.y_send, n.y_recv.at[d - 1], at.on_y(d)) for d in range(1, ny)]
    arrived(out_swap)
    for y in range(ny):
        total = n.outp[at.c, y]
        if nc > 1:
            total = total + n.oc_recv[y]
        n.outp[at.c, y] = total
        n.oy_send[y] = total.astype(BF)
    for d in range(1, ny):
        forward_x(d)
    io.sent(swap)
    arrived(sum_far)
    total = n.y_send[...].astype(F32)
    for d in range(1, ny):
        total = total + n.y_recv[d - 1].astype(F32)
    n.share[...] = total
    share = io.put_core(n.share, n.s_recv)

    def residual_back(ref, base):
        def step(from_rows, carry):
            rows = pl.ds(pl.multiple_of(base + from_rows.start, 16), 16)
            grad = ref[from_rows]
            hat, inv = n.hat[rows], n.inv[rows, 0:1]
            n.part[rows] = grad
            scaled = grad * n.vecs[4:5]
            first = jnp.mean(scaled, axis=-1, keepdims=True)
            second = jnp.mean(scaled * hat, axis=-1, keepdims=True)
            d_res = n.dout[rows].astype(F32) + inv * (scaled - first - hat * second)
            n.resid[rows] = d_res
            n.dattn[rows] = d_res.astype(BF)
            return carry

        sweep(0, half, step)

    n.own[0] = n.outp[at.c, at.y] + own_rows(n.resid)
    io.move(n.own.at[0], n.out_o)
    io.move(n.oy_send, n.out_send_o)
    residual_back(n.share, at.c * half)
    if nc > 1:
        arrived(share)
        residual_back(n.s_recv, (nc - 1 - at.c) * half)
    io.move(n.dattn, n.dattn_o)
    n.own[1] = own_rows(n.resid)
    io.move(n.own.at[1], n.dres_o)
    grad = own_rows(n.part)
    n.fvec[0:1] = jnp.sum(grad * own_rows(n.hat), axis=0, keepdims=True)
    n.fvec[1:2] = jnp.sum(grad, axis=0, keepdims=True)
    n.fvec[2:8] = jnp.zeros((6, D), F32)
    io.move(n.fvec, n.fvec_o)
    for d in range(ny):
        arrived(x_far[d])
    arrived(ffn_far)
    io.finish()


def call(kernel, s, name, ident, ins, outs, scratch, semaphores, places, limit, cost):
    names = list(ins) + list(outs) + list(scratch) + ["send", "recv", "local"]
    dma = [pltpu.SemaphoreType.DMA((count,)) for count in (semaphores, semaphores, 120)]
    result = pl.pallas_call(
        functools.partial(kernel, s, names),
        name=name,
        out_shape=[jax.ShapeDtypeStruct(*o) for o in outs.values()],
        in_specs=[places.get(k, ANY) for k in ins],
        out_specs=[ANY] * len(outs),
        scratch_shapes=[pltpu.VMEM(*v) for v in scratch.values()] + dma,
        compiler_params=pltpu.CompilerParams(collective_id=ident, has_side_effects=True, vmem_limit_bytes=limit << 20),
        cost_estimate=cost,
    )(*ins.values())
    return dict(zip(outs, result, strict=True))


def forward(s, ins):
    t = sizes_of(s)
    ny, nc, G, H, M, L, LR, GL, ML, D, E, F = t.ny, t.nc, t.G, t.H, t.M, t.L, t.LR, t.GL, t.ML, t.D, t.E, t.F
    half = GL // nc
    far = max(ny - 1, 1)
    outs = dict(
        out_o=((L, D), F32), dres_o=((L, D), F32), fvec_o=((8, D), F32), key_norm_o=((H * ML, D), BF),
        keys_o=((G, t.KC, E), BF), values_o=((G, t.KC, E), BF), query_o=((G, LR, E), BF), mixed_o=((H, GL, E), BF),
        dattn_o=((GL, D), BF), ffn_o=((GL, D), BF), dout_o=((GL, D), BF), act_o=((GL, F), BF), dhid_o=((GL, F), BF),
        dall=((s.rows, ny * L, D), BF), fall=((t.nz, L, D), BF), out_send_o=((ny, L, D), BF),
    )
    scratch = dict(
        vecs=((8, D), F32), cot_v=((L, D), BF), wide_l=((L, D), F32), raw_m=((H, M, D), BF), raw_l=((H * L, D), BF), dslot=((ny, nc, L, D), BF),
        norm=((2, M, D), BF), lnorm=((H * L, D), BF), turn=((GL, E), F32), keys=((G, t.KC, E), BF), values=((G, t.KC, E), BF),
        query=((G, LR, E), BF), mix=((H, GL, E), BF), resid=((GL, D), F32), hat=((GL, D), F32), inv=((GL, 128), F32),
        ffn=((GL, D), BF), dout=((GL, D), BF), act=((GL, F), BF), dhid=((GL, F), BF), part=((GL, D), F32),
        outp=((nc, ny, L, D), F32), c_recv=((half, D), F32), oc_recv=((ny, L, D), F32), y_send=((half, D), BF),
        y_recv=((far, half, D), BF), oy_send=((ny, L, D), BF), share=((half, D), F32),
        s_recv=((half, D), F32), fq=((L, D), BF), own=((2, L, D), F32), dattn=((GL, D), BF),
        fvec=((8, D), F32), wq_v=((D, E), BF), wk_v=((D, E), BF), wv_v=((D, E), BF), wout_v=((D, D), BF),
        wup_v=((D, F), BF), wdown_v=((F, D), BF),
    )
    places = {"counts": SMEM}
    cost = pl.CostEstimate(flops=8 * 10**9, bytes_accessed=4 * 10**7, transcendentals=10**6)
    return call(forward_kernel, s, "forward", 1, ins, outs, scratch, 200, places, 62, cost)


def window_of(position, block, width):
    base = jnp.minimum(position * block // 128 * 128, width - 256)
    return pl.multiple_of(base, 128), position * block - base


def backward_kernel(s, names, *refs):
    n = types.SimpleNamespace(**dict(zip(names, refs, strict=True)))
    at = Place(s.rows, s.heads)
    t = sizes_of(s)
    ny, nc, nz, nx, G, H = t.ny, t.nc, t.nz, t.nx, t.G, t.H
    M, L, LR, GL, ML, D, E, F, ll, pr, B = t.M, t.L, t.LR, t.GL, t.ML, t.D, t.E, t.F, t.ll, t.pr, t.B
    here = at.r
    io = Copies(at, n.send, n.recv, n.local)

    def quarter(r, y):
        return r, pl.ds(pl.multiple_of((at.c * ny + y) * L, 16), L)

    aligned = t.aligned
    first_loads = [io.move(n.dattn, n.ffn_v.at[1]), io.move(n.mixed, n.mix_v)]
    first_loads.append(io.move(n.wout.at[pl.ds(pl.multiple_of(at.h * E, 16), E)], n.wout_v))
    if aligned:
        first_loads.append(io.move(n.dattn.at[:, pl.ds(pl.multiple_of(at.h * E, 128), E)], n.dcols_v))
    else:
        first_loads.append(io.move(n.dattn_cols, n.dcols_v))
    attend_loads = [io.move(getattr(n, k), getattr(n, k + "_v")) for k in ("keys", "values", "query")]
    norm_load = io.move(n.key_norm, n.norm_v)
    own_loads = [io.move(n.act, n.dout_v.at[1, :, 0:F]), io.move(n.ffn, n.ffn_v.at[0]), io.move(n.dout, n.dout_v.at[0])]
    ffn_loads = [io.move(n.wup.at[:, pl.ds(pl.multiple_of(at.h * F, 128), F)], n.wup_v)]
    ffn_loads.append(io.move(n.wdown.at[pl.ds(pl.multiple_of(at.h * F, 16), F)], n.wdown_v))
    if aligned:
        row_loads = []
        for head in range(H):
            for j, weight in enumerate((n.wk, n.wv)):
                lanes = slice((2 * head + j) * E, (2 * head + j + 1) * E)
                row_loads.append(io.move(weight.at[:, head * E : (head + 1) * E], n.w_v.at[:, lanes]))
    else:
        row_loads = [io.move(n.wkv, n.w_v)]
    row_loads += [io.move(n.media_gain, n.vecs.at[0]), io.move(n.latent_gain, n.vecs.at[1]), io.move(n.out_own, n.out_own_v)]
    row_loads += [io.move(n.media, n.media_v), io.move(n.lat, n.lat_v), io.move(n.dres, n.dres_v)]
    at.greet()

    x_quarters = []
    for dz in range(nz):
        source = n.fall.at[lax.rem(at.z + dz, nz)]
        x_quarters.append(io.put_x(source, n.fall_b.at[quarter(at.group(dz, 0), at.y)]))
    y_quarters = {}
    for dz in range(1, nz):
        source = n.fall.at[lax.rem(at.z + dz, nz)]
        y_quarters[dz, 0] = io.put_y(source, n.fall_b.at[quarter(at.group(dz, 0), at.y)])

    def core_rows(c):
        return pl.ds(pl.multiple_of(c * ny * L, 16), ny * L)

    for dx in range(1, nx):
        for dz in range(nz):
            block = n.fall_b.at[quarter(at.group(dz, nx - dx), at.y)]
            y_quarters[dz, nx - dx] = [io.plan(block, block, at.on_y(d)) for d in range(1, ny)]
    order = [(dz, 0) for dz in range(1, nz)] + [(dz, nx - dx) for dx in range(1, nx) for dz in range(nz)]
    near, count = nz - 1, len(order)
    to_core, fetched = [], []
    for index, (dz, dx) in enumerate(order):
        r = at.group(dz, dx)
        buf = (index + 1) % 2
        copies = [io.plan(n.dall.at[r], n.dall_b.at[r], at.partner())] if nc > 1 else []
        for d in range(ny):
            block = n.fall_b.at[quarter(r, at.y_peer(d))]
            source = n.fall.at[lax.rem(at.z + dz, nz)] if (d == 0 and dx == 0) else block
            copies += [io.plan(source, block, at.partner())] if nc > 1 else []
        to_core.append(copies)
        copies = []
        for c in range(nc):
            rows = core_rows(at.c if c == 0 else nc - 1 - at.c)
            source = n.dall if c == 0 else n.dall_b
            copies.append(io.plan_move(source.at[r], n.dout_v.at[buf, rows]))
        if dx > 0:
            copies.append(io.plan_move(n.fall_b.at[r], n.ffn_v.at[buf]))
        else:
            for slot in range(H):
                head = at.head_of(slot)
                rows = pl.ds(pl.multiple_of((head % nc * ny + head // nc) * L, 16), L)
                source = n.fall.at[lax.rem(at.z + dz, nz)] if slot == 0 else n.fall_b.at[r, rows]
                copies.append(io.plan_move(source, n.ffn_v.at[buf, rows]))
        fetched.append(copies)

    def spread(index):
        arrived(y_quarters[order[index]])
        begin(to_core[index])

    def fetch(index):
        if index < count:
            arrived(to_core[index])
            begin(fetched[index])

    io.moved(*first_loads)
    n.dmixed[...] = mt(n.ffn_v[1], n.wout_v[...]).astype(BF).reshape(G, LR, E)
    own_loads.append(io.move(n.dhid, n.ffn_v.at[1, :, 0:F]))
    span = nx * B
    if E == span:
        tiles = [tm(n.mix_v[z], n.dcols_v[...]) for z in range(nz)]
    else:
        whole = jnp.concatenate([n.mix_v[head] for head in range(H)], axis=-1)
        tiles = [tm(whole[:, z * span : (z + 1) * span], n.dcols_v[...]) for z in range(nz)]
    for z in range(nz):
        for x in range(nx):
            n.p_out[z, x] = tiles[z][x * B : (x + 1) * B].astype(BF)
    out_x = [io.plan(n.p_out.at[at.z, lax.rem(at.x + d, nx)], n.xr_out.at[d - 1], at.on_x(d)) for d in range(1, nx)]
    out_z = [io.put(n.p_out.at[lax.rem(at.z + d, nz)], n.zr_out.at[d - 1], at.on_z(d)) for d in range(1, nz)]

    def out_middle():
        arrived(out_z)
        total = n.p_out[at.z].astype(F32)
        for d in range(1, nz):
            total = total + n.zr_out[d - 1].astype(F32)
        n.p_out[at.z] = total.astype(BF)
        begin(out_x)

    def out_end():
        arrived(out_x)
        total = n.p_out[at.z, at.x].astype(F32)
        for d in range(1, nx):
            total = total + n.xr_out[d - 1].astype(F32)
        n.grad_v[0] = total
        io.move(n.grad_v.at[0], n.out_grad)

    parts = {"kv": (n.p_kv, n.xr_kv, n.zr_kv), "query": (n.p_query, n.xr_query, n.zr_query)}
    x_parts, z_parts = {}, {}
    z_order = list(range(1, nz)) + [0]

    def sum_start(w, rows, grads):
        part, x_recv = parts[w][:2]
        for dz in z_order:
            lanes = pl.ds(pl.multiple_of(lax.rem(at.z + dz, nz) * span, 128), span)
            tile = tm(rows(lanes), grads)
            for x in range(nx):
                part[dz, x] = tile[x * B : (x + 1) * B].astype(BF)
            z_parts[w, dz] = [io.plan(part.at[dz, at.x], parts[w][2].at[dz - 1], at.on_z(dz))] if dz else []
            x_parts[w, dz] = [
                io.put(part.at[dz, lax.rem(at.x + d, nx)], x_recv.at[dz, d - 1], at.on_x(d)) for d in range(1, nx)
            ]

    def sum_middle(w, dz):
        part, x_recv, _ = parts[w]
        arrived(x_parts[w, dz])
        total = part[dz, at.x].astype(F32)
        for d in range(1, nx):
            total = total + x_recv[dz, d - 1].astype(F32)
        part[dz, at.x] = total.astype(BF)
        begin(z_parts[w, dz])

    def sum_end(w, outs):
        part, _, z_recv = parts[w]
        total = part[0, at.x].astype(F32)
        for dz in range(1, nz):
            arrived(z_parts[w, dz])
            total = total + z_recv[dz - 1].astype(F32)
        for j, (ref, out) in enumerate(outs):
            ref[...] = total[:, j * E : (j + 1) * E]
            io.move(ref, out)

    io.moved(*attend_loads)
    mask = head_mask(t.heads_here, LR, E)
    mask_low = mask.astype(BF)
    scale = 1.0 / math.sqrt(HEAD_DIM)
    for i in range(G):
        q = spread_heads(n.query_v[i], mask_low)
        d = spread_heads(n.dmixed[i], mask_low)
        k, v = n.keys_v[i], n.values_v[i]
        probs = softmax(mt(q, k) * scale)
        d_probs = mt(d, v)
        inner = jnp.sum(probs * d_probs, axis=-1, keepdims=True)
        d_scores = (probs * (d_probs - inner)).astype(BF)
        d_query = gather_heads(mm(d_scores, k), mask, LR) * scale
        d_pair = jnp.concatenate([tm(d_scores, q) * scale, tm(probs.astype(BF), d)], axis=-1)
        for slot in range(H):
            rows = slice(slot * ML + i * pr, slot * ML + (i + 1) * pr)
            n.dkv[rows] = d_pair[slot * pr : (slot + 1) * pr].astype(BF)
        for head in range(H):
            rows = slice(H * pr + head * ll, H * pr + (head + 1) * ll)
            n.turn_kv[head, i * ll : (i + 1) * ll] = d_pair[rows]
            n.turn_q[head, i * ll : (i + 1) * ll, 0:E] = d_query[head * ll : (head + 1) * ll]
    if t.EP > E:
        n.turn_q[:, :, E : t.EP] = jnp.zeros((H, L, t.EP - E), F32)
    for slot in range(H):
        head = at.head_of(slot)
        n.dkv[slot * ML + M : (slot + 1) * ML] = n.turn_kv[head].astype(BF)
        n.dq[slot * L : (slot + 1) * L] = n.turn_q[head].astype(BF)
    kv_lanes = pl.ds(pl.multiple_of(at.h * 2 * E, 128), 2 * E)
    q_lanes = pl.ds(pl.multiple_of(at.h * t.EP, 128), t.EP)
    turned = []
    for slot in range(1, H):
        peer = (at.r, at.head_of(slot))
        turned.append(io.put(n.dkv.at[slot * ML : (slot + 1) * ML], n.dkv_full.at[:, kv_lanes], peer))
        turned.append(io.put(n.dq.at[slot * L : (slot + 1) * L], n.dq_full.at[:, q_lanes], peer))
    out_far = [io.put(n.out_send.at[at.y_peer(d)], n.out_recv.at[d - 1], at.on_y(d)) for d in range(1, ny)]
    io.moved(norm_load)
    sum_start("kv", lambda lanes: n.norm_v[:, lanes], n.dkv[...])
    sum_start(
        "query",
        lambda lanes: jnp.concatenate([n.norm_v[slot * ML + M : (slot + 1) * ML, lanes] for slot in range(H)], axis=0),
        n.dq[:, 0:E],
    )
    base, offset = window_of(here, B, D)
    window = pl.ds(base, 256)
    io.moved(*own_loads)
    n.up_acc[...] = tm(n.ffn_v[0, :, window], n.ffn_v[1, :, 0:F])
    n.down_acc[...] = tm(n.dout_v[0, :, window], n.dout_v[1, :, 0:F])
    q_load = io.plan_move(n.wq, n.w_v.at[:, 0 : n.wq.shape[1]])
    media_out, lat_out = io.plan_move(n.drow.at[0:M], n.media_o), io.plan_move(n.drow.at[M:ML], n.lat_o)
    own_out = io.plan_move(n.out_own_v, n.out_o)
    vec_head = [io.plan(n.vec_own, n.vec_head.at[k - 1], (at.r, lax.rem(at.h + k, H))) for k in range(1, H)]
    vec_z = [io.plan(n.vec_sum.at[lax.rem(at.z + d, nz)], n.vec_z.at[d - 1], at.on_z(d)) for d in range(1, nz)]

    def norm_back_rows(raw, size, base, gain_row, extra):
        def step(rows, sums):
            grad_rows = pl.ds(pl.multiple_of(base + rows.start, 16), 16)
            hat, inv = norm_rows(raw[rows].astype(F32))
            grad = n.drow[grad_rows]
            product = grad * hat
            scaled = grad * n.vecs[gain_row : gain_row + 1]
            mean = jnp.mean(scaled, axis=-1, keepdims=True)
            second = jnp.mean(scaled * hat, axis=-1, keepdims=True)
            result = inv * (scaled - mean - hat * second)
            n.drow[grad_rows] = result if extra is None else result + extra[rows]
            return sums[0] + product[:8] + product[8:], sums[1] + grad[:8] + grad[8:]

        sums = sweep(0, size, step, (jnp.zeros((8, D), F32), jnp.zeros((8, D), F32)))
        return [jnp.sum(v, axis=0, keepdims=True) for v in sums]

    def own_gradients():
        n.dkv_full[:, kv_lanes] = n.dkv[0:ML]
        n.dq_full[:, q_lanes] = n.dq[0:L]
        io.moved(*row_loads)
        arrived(turned)
        n.drow[...] = mt(n.dkv_full[...], n.w_v[...])
        begin([q_load])
        n.vec_own[0:1], n.vec_own[1:2] = norm_back_rows(n.media_v, M, 0, 0, None)
        begin([media_out])
        io.moved(q_load)
        n.drow[M:ML] += mt(n.dq_full[...], n.w_v[:, 0 : n.wq.shape[1]])
        n.vec_own[2:3], n.vec_own[3:4] = norm_back_rows(n.lat_v, L, M, 1, n.dres_v)
        begin([lat_out])
        n.vec_own[4:6] = n.fvec[0:2]
        n.vec_own[6:8] = jnp.zeros((2, D), F32)
        begin(vec_head)

    def vectors_middle():
        arrived(vec_head)
        total = n.vec_own[...]
        for k in range(1, H):
            total = total + n.vec_head[k - 1]
        for z in range(nz):
            n.vec_sum[z] = total[:, z * span : (z + 1) * span]
        begin(vec_z)

    def own_output():
        arrived(out_far)
        total = n.out_own_v[...]
        for d in range(1, ny):
            total = total + n.out_recv[d - 1].astype(F32)
        n.out_own_v[...] = total
        begin([own_out])

    before = {index: [lambda index=index: io.moved(*fetched[index]), lambda index=index: fetch(index + 1)] for index in range(count)}
    after = {index: [] for index in range(count)}
    del before[near - 1][1:]

    def late_quarters():
        for dz, dx in order[near:]:
            arrived([x_quarters[dz][nx - dx - 1]])
            begin(y_quarters[dz, dx])

    after[0] += [late_quarters]
    after[near - 1] += [lambda: sum_middle("kv", z_order[0]), out_middle]
    after[near - 1] += [lambda dz=dz: sum_middle("kv", dz) for dz in z_order[1:2]]
    after[near - 1] += [own_gradients]
    after[near - 1] += [lambda dz=dz: sum_middle("kv", dz) for dz in z_order[2:]]
    after[near - 1] += [own_output]
    after[near - 1] += [lambda index=index: spread(index) for index in range(near, count)]
    after[near - 1] += [lambda: fetch(near)]
    late = list(range(near + 1, count)) or [count - 1]
    after[late[0]] += [lambda: sum_middle("query", z_order[0])]
    after[late[min(1, len(late) - 1)]] += [vectors_middle]
    for dz in z_order[1:]:
        after[late[min(dz, len(late) - 1)] if dz else late[-1]] += [lambda dz=dz: sum_middle("query", dz)]
    for index in range(near):
        spread(index)
    fetch(0)
    io.moved(*ffn_loads)

    def at_index(index, actions):
        for k in range(count):
            if actions[k]:

                @pl.when(index == k)
                def _():
                    for action in actions[k]:
                        action()

    def group_step(index, carry):
        at_index(index, before)
        buf = lax.rem(index + 1, 2)
        value, slope = gelu_pair(mm(n.ffn_v[buf], n.wup_v[...]))
        d_hidden = (mt(n.dout_v[buf], n.wdown_v[...]) * slope).astype(BF)
        n.up_acc[...] += tm(n.ffn_v[buf, :, window], d_hidden)
        n.down_acc[...] += tm(n.dout_v[buf, :, window], value.astype(BF))
        at_index(index, after)
        return carry

    lax.fori_loop(0, count, group_step, 0)
    arrived(vec_z)
    total = n.vec_sum[at.z]
    for d in range(1, nz):
        total = total + n.vec_z[d - 1]
    n.vec_part[...] = total
    vec_x = [io.put(n.vec_part, n.vec_x.at[d - 1], at.on_x(d)) for d in range(1, nx)]
    own_rows = pl.ds(pl.multiple_of(offset, 8), B)
    io.move(n.up_acc.at[own_rows], n.up_grad)
    io.move(n.down_acc.at[own_rows], n.down_grad)
    out_end()
    sum_end("kv", [(n.grad_v.at[1], n.key_grad), (n.grad_v.at[2], n.value_grad)])
    arrived(vec_x)
    total = n.vec_part[...]
    for d in range(1, nx):
        total = total + n.vec_x[d - 1]
    n.vec_done[...] = total
    io.move(n.vec_done, n.vec_o)
    sum_end("query", [(n.grad_v.at[3], n.query_grad)])
    io.finish()


def backward(s, ins):
    t = sizes_of(s)
    ny, nc, nz, nx, G, H = t.ny, t.nc, t.nz, t.nx, t.G, t.H
    M, L, LR, GL, ML, D, E, F, B = t.M, t.L, t.LR, t.GL, t.ML, t.D, t.E, t.F, t.B
    fx, fz, fh = max(nx - 1, 1), max(nz - 1, 1), max(H - 1, 1)
    span = D // nz
    outs = dict(
        media_o=((M, D), F32), lat_o=((L, D), F32), query_grad=((B, E), F32), key_grad=((B, E), F32), value_grad=((B, E), F32),
        out_grad=((B, E), F32), up_grad=((B, F), F32), down_grad=((B, F), F32), vec_o=((8, span), F32), out_o=((L, D), F32),
        fall_b=((s.rows, GL, D), BF), dall_b=((s.rows, ny * L, D), BF),
    )
    scratch = dict(
        mix_v=((H, GL, E), BF), wout_v=((E, D), BF), dcols_v=((GL, E), BF), dmixed=((G, LR, E), BF),
        keys_v=((G, t.KC, E), BF), values_v=((G, t.KC, E), BF), query_v=((G, LR, E), BF), norm_v=((H * ML, D), BF),
        ffn_v=((2, GL, D), BF), dout_v=((2, GL, D), BF), wup_v=((D, F), BF),
        wdown_v=((F, D), BF), w_v=((D, max(2 * D, H * t.EP)), BF), media_v=((M, D), BF), lat_v=((L, D), BF), dres_v=((L, D), F32),
        dkv=((H * ML, 2 * E), BF), dq=((H * L, t.EP), BF), turn_kv=((H, L, 2 * E), F32), turn_q=((H, L, t.EP), F32),
        dkv_full=((ML, 2 * D), BF), dq_full=((L, H * t.EP), BF), grad_v=((4, B, E), F32), up_acc=((256, F), F32),
        down_acc=((256, F), F32), drow=((ML, D), F32), vec_own=((8, D), F32), vec_head=((fh, 8, D), F32),
        vec_sum=((nz, 8, span), F32), vec_z=((fz, 8, span), F32), vec_part=((8, span), F32), vec_x=((fx, 8, span), F32),
        vec_done=((8, span), F32), vecs=((8, D), F32), out_own_v=((L, D), F32), out_recv=((max(ny - 1, 1), L, D), BF),
        p_out=((nz, nx, B, E), BF), zr_out=((fz, nx, B, E), BF), xr_out=((fx, B, E), BF),
    )
    for w, lanes in (("kv", 2 * E), ("query", E)):
        scratch["p_" + w] = ((nz, nx, B, lanes), BF)
        scratch["xr_" + w] = ((nz, fx, B, lanes), BF)
        scratch["zr_" + w] = ((fz, B, lanes), BF)
    places = {"fvec": VMEM}
    cost = pl.CostEstimate(flops=30 * 10**9, bytes_accessed=8 * 10**7, transcendentals=10**6)
    return call(backward_kernel, s, "backward", 2, ins, outs, scratch, 300, places, 63, cost)


def finish_kernel(count, *refs):
    ins, outs, held = refs[:count], refs[count : 2 * count], refs[2 * count : 3 * count]
    read, write = refs[3 * count :]
    loads = [pltpu.make_async_copy(a, b, read.at[i]) for i, (a, b) in enumerate(zip(ins, held))]
    stores = [pltpu.make_async_copy(a, b, write.at[i]) for i, (a, b) in enumerate(zip(held, outs))]
    for copy in loads:
        copy.start()
    for load, store in zip(loads, stores):
        load.wait()
        store.start()
    for copy in stores:
        copy.wait()


def finish(arrays):
    count = len(arrays)
    return pl.pallas_call(
        functools.partial(finish_kernel, count),
        name="finish",
        out_shape=[jax.ShapeDtypeStruct(a.shape, a.dtype) for a in arrays],
        in_specs=[ANY] * count,
        out_specs=[ANY] * count,
        scratch_shapes=[pltpu.VMEM(a.shape, a.dtype) for a in arrays] + [pltpu.SemaphoreType.DMA((count,))] * 2,
        compiler_params=pltpu.CompilerParams(vmem_limit_bytes=62 << 20),
    )(*arrays)


def body(
    media, latents, counts, media_gain, media_shift, latent_gain, latent_shift, w_query, w_key, w_value, w_out,
    ffn_gain, ffn_shift, w_up, w_down, cotangent,
):
    rows, heads = lax.axis_size("rows"), lax.axis_size("head")
    at = Place(rows, heads)
    images, patch, width = media.shape
    lat = latents.shape[1]
    cols = width // heads
    s = types.SimpleNamespace(
        rows=rows, heads=heads, images=images, patch=patch, lat=lat, width=width, cols=cols, mine=w_up.shape[1] // heads
    )
    t = sizes_of(s)

    def columns(array):
        return array if t.aligned else lax.dynamic_slice_in_dim(array, at.h * cols, cols, 1)

    gains = dict(
        media_gain=media_gain, media_shift=media_shift, latent_gain=latent_gain, latent_shift=latent_shift,
        ffn_gain=ffn_gain, ffn_shift=ffn_shift,
    )
    rows_in = dict(media=media.reshape(-1, width), lat=latents.reshape(-1, width))
    a = forward(
        s,
        dict(
            rows_in, cot=cotangent.reshape(-1, width), counts=counts, **gains, wq=columns(w_query), wk=columns(w_key),
            wv=columns(w_value), wout=w_out, wup=w_up, wdown=w_down,
        ),
    )
    ins = dict(
        rows_in, media_gain=gains["media_gain"], latent_gain=gains["latent_gain"], fvec=a["fvec_o"], dres=a["dres_o"],
        key_norm=a["key_norm_o"], keys=a["keys_o"], values=a["values_o"], query=a["query_o"], mixed=a["mixed_o"],
        dattn=a["dattn_o"], ffn=a["ffn_o"], dout=a["dout_o"], act=a["act_o"], dhid=a["dhid_o"], dall=a["dall"], fall=a["fall"],
        wout=w_out, wup=w_up, wdown=w_down, out_own=a["out_o"], out_send=a["out_send_o"],
    )
    if t.aligned:
        ins.update(wk=w_key, wv=w_value, wq=w_query)
    else:
        pair = jnp.stack([w_key.reshape(width, heads, cols), w_value.reshape(width, heads, cols)], axis=2)
        padded = jnp.pad(w_query.reshape(width, heads, cols), ((0, 0), (0, 0), (0, t.EP - cols)))
        ins.update(wkv=pair.reshape(width, 2 * width), wq=padded.reshape(width, -1), dattn_cols=columns(a["dattn_o"]))
    b = backward(s, ins)
    share = width // (rows * heads)
    vector = lax.dynamic_slice_in_dim(b["vec_o"], (at.x * heads + at.h) * share, share, 1)
    names = ("out_o", "media_o", "lat_o", "query_grad", "key_grad", "value_grad", "out_grad", "up_grad", "down_grad")
    out, media_grad, latents_grad, query_grad, key_grad, value_grad, out_grad, up_grad, down_grad = finish([b[k] for k in names])
    return (
        out.reshape(latents.shape), media_grad.reshape(media.shape), latents_grad.reshape(latents.shape), vector[0], vector[1],
        vector[2], vector[3], query_grad, key_grad, value_grad, out_grad, vector[4], vector[5], up_grad, down_grad.T,
    )


def solution(mesh):
    row = P("rows", "head", None)
    whole = P()
    vector = P(("rows", "head"))
    grid = P("rows", "head")
    return jax.shard_map(
        body,
        mesh=mesh,
        in_specs=(row, row) + (whole,) * 13 + (row,),
        out_specs=(row, row, row, vector, vector, vector, vector, grid, grid, grid, grid, vector, vector, grid, P("head", "rows")),
        check_vma=False,
    )
```

profile of v0, /device:TPU:0, one launch (start us, length us, event | category | flops | bytes accessed | tf_op | source)
XLA Modules:
  0.0 175.2 jit_solution(2946064377276915498)
XLA Ops:
  0.6 71.8 %forward.1 = (f32[64,1536]{1,0:T(8,128)}, f32[64,1536]{1,0:T(8,128)}, f32[8,1536]{1,0:T(8,128)}, bf16[1280,1536]{1,0:T(8,128)(2,1)}, bf16[4,320,384]{2,1,0:T(8,1...) custom-call(bf16[256,1536]{1,0:T(8,128)(2,1)} %bitcast.19, ...), custom_call_target="tpu_custom_call" | custom-call | flops 8000000000 | bytes 40000000 | tf_op jit(solution)/shard_map/forward/pallas_call | solution.py:514
  72.5 96.5 %backward.1 = (f32[256,1536]{1,0:T(8,128)}, f32[64,1536]{1,0:T(8,128)}, f32[192,384]{1,0:T(8,128)}, f32[192,384]{1,0:T(8,128)}, f32[192,384]{1,0:T(8,128)}, /*in...) custom-call(bf16[256,1536]{1,0:T(8,128)(2,1)} %bitcast.20, ...), custom_call_target="tpu_custom_call" | custom-call | flops 30000001024 | bytes 80000000 | tf_op jit(solution)/shard_map/backward/pallas_call | solution.py:514
  169.0 4.9 %finish.1 = (f32[64,1536]{1,0:T(8,128)}, f32[256,1536]{1,0:T(8,128)}, f32[64,1536]{1,0:T(8,128)}, f32[192,384]{1,0:T(8,128)}, f32[192,384]{1,0:T(8,128)}, /*inde...) custom-call(f32[64,1536]{1,0:T(8,128)} %get-tuple-element.66.refs_0_, ...), custom_call_target="tpu_custom_call" | custom-call | tf_op jit(solution)/shard_map/finish/pallas_call | solution.py:932
  173.9 0.8 constant_dynamic-slice_fusion
  174.7 0.5 slice_bitcast_fusion
where the time goes:
time: 176 us; the launch traced here: 175 us
  Pallas kernels  173 us (98%)
    pallas_call x2, Pallas kernels, call(): pl.pallas_call(functools.partial(kernel, s, names), name=name, out_shape=...  168 us
    pallas_call x1, Pallas kernels, finish(): pl.pallas_call(functools.partial(finish_kernel, count), name='finish', ou...  4.9 us

commit v1 on v0

--- a/solution.py
+++ b/solution.py
@@ -49,21 +49,29 @@
         self.ny, self.nc = factor_head(heads)
         self.r = lax.axis_index("rows")
         self.h = lax.axis_index("head")
-        self.z, self.x = self.r // self.nx, self.r % self.nx
-        self.y, self.c = self.h // self.nc, self.h % self.nc
-
-    def y_peer(self, d):
-        return lax.rem(self.y + d, self.ny)
+        self.z, self.x = lax.div(self.r, self.nx), lax.rem(self.r, self.nx)
+        self.y, self.c = lax.div(self.h, self.nc), lax.rem(self.h, self.nc)
+        self.zs, self.xs, self.ys = [
+            [self.turn(at, d, size) for d in range(size)]
+            for at, size in ((self.z, self.nz), (self.x, self.nx), (self.y, self.ny))
+        ]
+        self.other = self.nc - 1 - self.c
+        self.groups = [[z * self.nx + x for x in self.xs] for z in self.zs]
+        self.slots = [y * self.nc + c for y in self.ys for c in (self.c, self.other)[: self.nc]]
+        self.partner = (self.r, self.y * self.nc + self.other)
+
+    @staticmethod
+    def turn(at, d, size):
+        if d == 0:
+            return at
+        there = at + d
+        return jnp.where(there >= size, there - size, there)
 
     def group(self, dz, dx):
-        return lax.rem(self.z + dz, self.nz) * self.nx + lax.rem(self.x + dx, self.nx)
-
-    def head_of(self, slot):
-        d, e = divmod(slot, self.nc)
-        return self.y_peer(d) * self.nc + (self.c if e == 0 else self.nc - 1 - self.c)
+        return self.groups[dz % self.nz][dx % self.nx]
 
     def on_y(self, d):
-        return self.r, self.y_peer(d) * self.nc + self.c
+        return self.r, self.slots[d * self.nc]
 
     def on_x(self, d):
         return self.group(0, d), self.h
@@ -71,11 +79,8 @@
     def on_z(self, d):
         return self.group(d, 0), self.h
 
-    def partner(self):
-        return self.r, self.y * self.nc + (self.nc - 1 - self.c)
-
     def greet(self):
-        peers = [(self.r, lax.rem(self.h + d, self.heads)) for d in range(1, self.heads)]
+        peers = [(self.r, head) for head in self.slots[1:]]
         peers += [self.on_x(d) for d in range(1, self.nx)] + [self.on_z(d) for d in range(1, self.nz)]
         barrier = pltpu.get_barrier_semaphore()
         for peer in peers:
@@ -117,7 +122,7 @@
         return [self.put(src, dst, self.at.on_z(d)) for d in range(1, self.at.nz)]
 
     def put_core(self, src, dst):
-        return [self.put(src, dst, self.at.partner())] if self.at.nc > 1 else []
+        return [self.put(src, dst, self.at.partner)] if self.at.nc > 1 else []
 
     def sent(self, copies):
         for copy in copies:
@@ -191,10 +196,10 @@
 
 
 def head_mask(heads_here, rows, cols):
-    shape = (heads_here * rows, cols)
-    row = lax.broadcasted_iota(jnp.int32, shape, 0) // rows
-    col = lax.broadcasted_iota(jnp.int32, shape, 1) // HEAD_DIM
-    return (row == col).astype(F32)
+    col = lax.broadcasted_iota(jnp.int32, (rows, cols), 1)
+    return jnp.concatenate(
+        [((col >= j * HEAD_DIM) & (col < (j + 1) * HEAD_DIM)).astype(F32) for j in range(heads_here)], axis=0
+    )
 
 
 def spread_heads(block, mask):
@@ -261,7 +266,7 @@
     io.moved(load_cot)
     for i in range(G):
         image = here * G + i
-        limit = n.counts[image // MAX_IMG]
+        limit = n.counts[lax.div(image, MAX_IMG)]
         live = jnp.where(lax.rem(image, MAX_IMG) < limit, 1.0, 0.0).astype(F32)
         rows = slice(i * ll, (i + 1) * ll)
         n.wide_l[rows] = n.cot_v[rows].astype(F32) * live
@@ -284,7 +289,7 @@
     def forward_x(d):
         for dz, copy in enumerate(z_far[d], 1):
             copy.wait_recv()
-            block = n.dall.at[quarter(at.group(nz - dz, 0), at.y_peer(d))]
+            block = n.dall.at[quarter(at.group(nz - dz, 0), at.ys[d])]
             x_far[d] += io.put_x(block, block)
 
     norm_busy = {}
@@ -329,7 +334,7 @@
     for k in range(H):
         wide = n.raw_l[k * L : (k + 1) * L].astype(F32)
         for i in range(G):
-            n.resid[pl.ds(pl.multiple_of(i * LR + at.head_of(k) * ll, 8), ll)] = wide[i * ll : (i + 1) * ll]
+            n.resid[pl.ds(pl.multiple_of(i * LR + at.slots[k] * ll, 8), ll)] = wide[i * ll : (i + 1) * ll]
 
     def latent_step(rows, carry):
         hat, _ = norm_rows(n.raw_l[rows].astype(F32))
@@ -343,7 +348,7 @@
         wide = mm(n.lnorm[...], weight[...])
         for k in range(H):
             for i in range(G):
-                n.turn[pl.ds(pl.multiple_of(i * LR + at.head_of(k) * ll, 8), ll)] = wide[k * L + i * ll : k * L + (i + 1) * ll]
+                n.turn[pl.ds(pl.multiple_of(i * LR + at.slots[k] * ll, 8), ll)] = wide[k * L + i * ll : k * L + (i + 1) * ll]
         for i in range(G):
             block = n.turn[i * LR : (i + 1) * LR].astype(BF)
             if result is n.query:
@@ -364,6 +369,12 @@
             if nc > 1:
                 arrived(relays[d - 1])
                 patches(far_slot(d) + 1, j * part // 16, (j + 1) * part // 16)
+    arrived(cot_far)
+    cot_relay = []
+    for d in range(1, ny):
+        block = n.dslot.at[at.ys[d], at.c]
+        cot_relay += io.put_core(block, block)
+        z_far[d], x_far[d] = across(at.ys[d], block)
     forward_x(0)
     mask = head_mask(t.heads_here, LR, E)
     mask_low = mask.astype(BF)
@@ -383,15 +394,9 @@
         n.resid[...] += mm(n.mix[head], n.wout_v[pl.ds(pl.multiple_of(head * E, 16), E)])
 
     add_mixed(at.h)
-    arrived(cot_far)
-    cot_relay = []
-    for d in range(1, ny):
-        block = n.dslot.at[at.y_peer(d), at.c]
-        cot_relay += io.put_core(block, block)
-        z_far[d], x_far[d] = across(at.y_peer(d), block)
     arrived(mix_near)
     if nc > 1:
-        add_mixed(at.head_of(1))
+        add_mixed(at.slots[1])
     arrived(cot_near)
     arrived(cot_relay)
     for y in range(ny):
@@ -404,14 +409,14 @@
     mix_relay = []
     for d, copy in zip(range(1, ny), mix_far):
         copy.wait_recv()
-        block = n.mix.at[at.head_of(far_slot(d))]
+        block = n.mix.at[at.slots[far_slot(d)]]
         mix_relay.append(io.put_core(block, block))
     for d in range(1, ny):
-        add_mixed(at.head_of(far_slot(d)))
+        add_mixed(at.slots[far_slot(d)])
     for d in range(1, ny):
         if nc > 1:
             arrived(mix_relay[d - 1])
-            add_mixed(at.head_of(far_slot(d) + 1))
+            add_mixed(at.slots[far_slot(d) + 1])
     io.move(n.mix, n.mixed_o)
     gain, shift = n.vecs[4:5], n.vecs[5:6]
 
@@ -437,7 +442,6 @@
     n.dhid[...] = (mt(n.dout[...], n.wdown_v[...]) * slope).astype(BF)
     n.part[...] = mt(n.dhid[...], n.wup_v[...])
     half = GL // nc
-    mine = pl.ds(pl.multiple_of(at.c * half, 16), half)
     theirs = pl.ds(pl.multiple_of((nc - 1 - at.c) * half, 16), half)
     swap = io.put_core(n.part.at[theirs], n.c_recv)
     io.move(n.act, n.act_o)
@@ -449,11 +453,16 @@
             n.outp[head % nc, head // nc, i * ll : (i + 1) * ll] = out_part[base : base + ll]
     out_swap = io.put_core(n.outp.at[nc - 1 - at.c], n.oc_recv)
     arrived(swap)
-    total = n.part[mine]
-    if nc > 1:
-        total = total + n.c_recv[...]
-    n.y_send[...] = total.astype(BF)
-    sum_far = [io.put(n.y_send, n.y_recv.at[d - 1], at.on_y(d)) for d in range(1, ny)]
+    pieces = 2
+    piece = half // pieces
+    sum_far = []
+    for j in range(pieces):
+        rows = slice(j * piece, (j + 1) * piece)
+        total = n.part[pl.ds(pl.multiple_of(at.c * half + j * piece, 16), piece)]
+        if nc > 1:
+            total = total + n.c_recv[rows]
+        n.y_send[rows] = total.astype(BF)
+        sum_far.append([io.put(n.y_send.at[rows], n.y_recv.at[d - 1, rows], at.on_y(d)) for d in range(1, ny)])
     arrived(out_swap)
     for y in range(ny):
         total = n.outp[at.c, y]
@@ -464,14 +473,8 @@
     for d in range(1, ny):
         forward_x(d)
     io.sent(swap)
-    arrived(sum_far)
-    total = n.y_send[...].astype(F32)
-    for d in range(1, ny):
-        total = total + n.y_recv[d - 1].astype(F32)
-    n.share[...] = total
-    share = io.put_core(n.share, n.s_recv)
-
-    def residual_back(ref, base):
+
+    def residual_back(ref, base, first, last):
         def step(from_rows, carry):
             rows = pl.ds(pl.multiple_of(base + from_rows.start, 16), 16)
             grad = ref[from_rows]
@@ -485,15 +488,25 @@
             n.dattn[rows] = d_res.astype(BF)
             return carry
 
-        sweep(0, half, step)
+        sweep(first, last, step)
 
     n.own[0] = n.outp[at.c, at.y] + own_rows(n.resid)
     io.move(n.own.at[0], n.out_o)
     io.move(n.oy_send, n.out_send_o)
-    residual_back(n.share, at.c * half)
+    share = []
+    for j in range(pieces):
+        rows = slice(j * piece, (j + 1) * piece)
+        arrived(sum_far[j])
+        total = n.y_send[rows].astype(F32)
+        for d in range(1, ny):
+            total = total + n.y_recv[d - 1, rows].astype(F32)
+        n.share[rows] = total
+        share.append(io.put_core(n.share.at[rows], n.s_recv.at[rows]))
+        residual_back(n.share, at.c * half, j * piece, (j + 1) * piece)
     if nc > 1:
-        arrived(share)
-        residual_back(n.s_recv, (nc - 1 - at.c) * half)
+        for j in range(pieces):
+            arrived(share[j])
+            residual_back(n.s_recv, (nc - 1 - at.c) * half, j * piece, (j + 1) * piece)
     io.move(n.dattn, n.dattn_o)
     n.own[1] = own_rows(n.resid)
     io.move(n.own.at[1], n.dres_o)
@@ -594,11 +607,11 @@
 
     x_quarters = []
     for dz in range(nz):
-        source = n.fall.at[lax.rem(at.z + dz, nz)]
+        source = n.fall.at[at.zs[dz]]
         x_quarters.append(io.put_x(source, n.fall_b.at[quarter(at.group(dz, 0), at.y)]))
     y_quarters = {}
     for dz in range(1, nz):
-        source = n.fall.at[lax.rem(at.z + dz, nz)]
+        source = n.fall.at[at.zs[dz]]
         y_quarters[dz, 0] = io.put_y(source, n.fall_b.at[quarter(at.group(dz, 0), at.y)])
 
     def core_rows(c):
@@ -614,11 +627,11 @@
     for index, (dz, dx) in enumerate(order):
         r = at.group(dz, dx)
         buf = (index + 1) % 2
-        copies = [io.plan(n.dall.at[r], n.dall_b.at[r], at.partner())] if nc > 1 else []
+        copies = [io.plan(n.dall.at[r], n.dall_b.at[r], at.partner)] if nc > 1 else []
         for d in range(ny):
-            block = n.fall_b.at[quarter(r, at.y_peer(d))]
-            source = n.fall.at[lax.rem(at.z + dz, nz)] if (d == 0 and dx == 0) else block
-            copies += [io.plan(source, block, at.partner())] if nc > 1 else []
+            block = n.fall_b.at[quarter(r, at.ys[d])]
+            source = n.fall.at[at.zs[dz]] if (d == 0 and dx == 0) else block
+            copies += [io.plan(source, block, at.partner)] if nc > 1 else []
         to_core.append(copies)
         copies = []
         for c in range(nc):
@@ -629,9 +642,9 @@
             copies.append(io.plan_move(n.fall_b.at[r], n.ffn_v.at[buf]))
         else:
             for slot in range(H):
-                head = at.head_of(slot)
-                rows = pl.ds(pl.multiple_of((head % nc * ny + head // nc) * L, 16), L)
-                source = n.fall.at[lax.rem(at.z + dz, nz)] if slot == 0 else n.fall_b.at[r, rows]
+                core = at.c if slot % nc == 0 else at.other
+                rows = pl.ds(pl.multiple_of((core * ny + at.ys[slot // nc]) * L, 16), L)
+                source = n.fall.at[at.zs[dz]] if slot == 0 else n.fall_b.at[r, rows]
                 copies.append(io.plan_move(source, n.ffn_v.at[buf, rows]))
         fetched.append(copies)
 
@@ -656,8 +669,8 @@
     for z in range(nz):
         for x in range(nx):
             n.p_out[z, x] = tiles[z][x * B : (x + 1) * B].astype(BF)
-    out_x = [io.plan(n.p_out.at[at.z, lax.rem(at.x + d, nx)], n.xr_out.at[d - 1], at.on_x(d)) for d in range(1, nx)]
-    out_z = [io.put(n.p_out.at[lax.rem(at.z + d, nz)], n.zr_out.at[d - 1], at.on_z(d)) for d in range(1, nz)]
+    out_x = [io.plan(n.p_out.at[at.z, at.xs[d]], n.xr_out.at[d - 1], at.on_x(d)) for d in range(1, nx)]
+    out_z = [io.put(n.p_out.at[at.zs[d]], n.zr_out.at[d - 1], at.on_z(d)) for d in range(1, nz)]
 
     def out_middle():
         arrived(out_z)
@@ -682,13 +695,13 @@
     def sum_start(w, rows, grads):
         part, x_recv = parts[w][:2]
         for dz in z_order:
-            lanes = pl.ds(pl.multiple_of(lax.rem(at.z + dz, nz) * span, 128), span)
+            lanes = pl.ds(pl.multiple_of(at.zs[dz] * span, 128), span)
             tile = tm(rows(lanes), grads)
             for x in range(nx):
                 part[dz, x] = tile[x * B : (x + 1) * B].astype(BF)
             z_parts[w, dz] = [io.plan(part.at[dz, at.x], parts[w][2].at[dz - 1], at.on_z(dz))] if dz else []
             x_parts[w, dz] = [
-                io.put(part.at[dz, lax.rem(at.x + d, nx)], x_recv.at[dz, d - 1], at.on_x(d)) for d in range(1, nx)
+                io.put(part.at[dz, at.xs[d]], x_recv.at[dz, d - 1], at.on_x(d)) for d in range(1, nx)
             ]
 
     def sum_middle(w, dz):
@@ -734,17 +747,17 @@
     if t.EP > E:
         n.turn_q[:, :, E : t.EP] = jnp.zeros((H, L, t.EP - E), F32)
     for slot in range(H):
-        head = at.head_of(slot)
+        head = at.slots[slot]
         n.dkv[slot * ML + M : (slot + 1) * ML] = n.turn_kv[head].astype(BF)
         n.dq[slot * L : (slot + 1) * L] = n.turn_q[head].astype(BF)
     kv_lanes = pl.ds(pl.multiple_of(at.h * 2 * E, 128), 2 * E)
     q_lanes = pl.ds(pl.multiple_of(at.h * t.EP, 128), t.EP)
     turned = []
     for slot in range(1, H):
-        peer = (at.r, at.head_of(slot))
+        peer = (at.r, at.slots[slot])
         turned.append(io.put(n.dkv.at[slot * ML : (slot + 1) * ML], n.dkv_full.at[:, kv_lanes], peer))
         turned.append(io.put(n.dq.at[slot * L : (slot + 1) * L], n.dq_full.at[:, q_lanes], peer))
-    out_far = [io.put(n.out_send.at[at.y_peer(d)], n.out_recv.at[d - 1], at.on_y(d)) for d in range(1, ny)]
+    out_far = [io.plan(n.out_send.at[at.ys[d]], n.out_recv.at[d - 1], at.on_y(d)) for d in range(1, ny)]
     io.moved(norm_load)
     sum_start("kv", lambda lanes: n.norm_v[:, lanes], n.dkv[...])
     sum_start(
@@ -760,8 +773,12 @@
     q_load = io.plan_move(n.wq, n.w_v.at[:, 0 : n.wq.shape[1]])
     media_out, lat_out = io.plan_move(n.drow.at[0:M], n.media_o), io.plan_move(n.drow.at[M:ML], n.lat_o)
     own_out = io.plan_move(n.out_own_v, n.out_o)
-    vec_head = [io.plan(n.vec_own, n.vec_head.at[k - 1], (at.r, lax.rem(at.h + k, H))) for k in range(1, H)]
-    vec_z = [io.plan(n.vec_sum.at[lax.rem(at.z + d, nz)], n.vec_z.at[d - 1], at.on_z(d)) for d in range(1, nz)]
+    vec_z = [io.plan(n.vec_sum.at[at.zs[d]], n.vec_z.at[d - 1], at.on_z(d)) for d in range(1, nz)]
+
+    def back_slot(k):
+        return (ny - k // nc) % ny * nc + k % nc
+
+    vec_head = [io.plan(n.vec_own, n.vec_head.at[back_slot(k) - 1], (at.r, at.slots[k])) for k in range(1, H)]
 
     def norm_back_rows(raw, size, base, gain_row, extra):
         def step(rows, sums):
@@ -795,6 +812,7 @@
         n.vec_own[4:6] = n.fvec[0:2]
         n.vec_own[6:8] = jnp.zeros((2, D), F32)
         begin(vec_head)
+        begin(out_far)
 
     def vectors_middle():
         arrived(vec_head)
@@ -813,30 +831,30 @@
         n.out_own_v[...] = total
         begin([own_out])
 
-    before = {index: [lambda index=index: io.moved(*fetched[index]), lambda index=index: fetch(index + 1)] for index in range(count)}
-    after = {index: [] for index in range(count)}
-    del before[near - 1][1:]
+    before, middle, after = [{index: [] for index in range(count)} for _ in range(3)]
 
     def late_quarters():
         for dz, dx in order[near:]:
             arrived([x_quarters[dz][nx - dx - 1]])
             begin(y_quarters[dz, dx])
 
-    after[0] += [late_quarters]
+    for index in range(count):
+        before[index] += [lambda index=index: io.moved(*fetched[index])]
+        if index + 1 < count and index != near - 1:
+            before[index] += [lambda index=index: spread(index + 1)]
+            middle[index] += [lambda index=index: fetch(index + 1)]
+    middle[0] += [late_quarters]
     after[near - 1] += [lambda: sum_middle("kv", z_order[0]), out_middle]
     after[near - 1] += [lambda dz=dz: sum_middle("kv", dz) for dz in z_order[1:2]]
     after[near - 1] += [own_gradients]
     after[near - 1] += [lambda dz=dz: sum_middle("kv", dz) for dz in z_order[2:]]
-    after[near - 1] += [own_output]
-    after[near - 1] += [lambda index=index: spread(index) for index in range(near, count)]
-    after[near - 1] += [lambda: fetch(near)]
-    late = list(range(near + 1, count)) or [count - 1]
-    after[late[0]] += [lambda: sum_middle("query", z_order[0])]
+    after[near - 1] += [lambda: spread(near), lambda: fetch(near)]
+    late = list(range(near, count))
     after[late[min(1, len(late) - 1)]] += [vectors_middle]
-    for dz in z_order[1:]:
-        after[late[min(dz, len(late) - 1)] if dz else late[-1]] += [lambda dz=dz: sum_middle("query", dz)]
-    for index in range(near):
-        spread(index)
+    for position, dz in enumerate(z_order):
+        after[late[min(position + 1, len(late) - 1)]] += [lambda dz=dz: sum_middle("query", dz)]
+    after[late[-1]] += [own_output]
+    spread(0)
     fetch(0)
     io.moved(*ffn_loads)
 
@@ -853,9 +871,11 @@
         at_index(index, before)
         buf = lax.rem(index + 1, 2)
         value, slope = gelu_pair(mm(n.ffn_v[buf], n.wup_v[...]))
-        d_hidden = (mt(n.dout_v[buf], n.wdown_v[...]) * slope).astype(BF)
+        n.down_acc[...] += tm(n.dout_v[buf, :, window], value.astype(BF))
+        n.slope[...] = slope
+        at_index(index, middle)
+        d_hidden = (mt(n.dout_v[buf], n.wdown_v[...]) * n.slope[...]).astype(BF)
         n.up_acc[...] += tm(n.ffn_v[buf, :, window], d_hidden)
-        n.down_acc[...] += tm(n.dout_v[buf, :, window], value.astype(BF))
         at_index(index, after)
         return carry
 
@@ -899,7 +919,7 @@
         wdown_v=((F, D), BF), w_v=((D, max(2 * D, H * t.EP)), BF), media_v=((M, D), BF), lat_v=((L, D), BF), dres_v=((L, D), F32),
         dkv=((H * ML, 2 * E), BF), dq=((H * L, t.EP), BF), turn_kv=((H, L, 2 * E), F32), turn_q=((H, L, t.EP), F32),
         dkv_full=((ML, 2 * D), BF), dq_full=((L, H * t.EP), BF), grad_v=((4, B, E), F32), up_acc=((256, F), F32),
-        down_acc=((256, F), F32), drow=((ML, D), F32), vec_own=((8, D), F32), vec_head=((fh, 8, D), F32),
+        down_acc=((256, F), F32), drow=((ML, D), F32), slope=((GL, F), F32), vec_own=((8, D), F32), vec_head=((fh, 8, D), F32),
         vec_sum=((nz, 8, span), F32), vec_z=((fz, 8, span), F32), vec_part=((8, span), F32), vec_x=((fx, 8, span), F32),
         vec_done=((8, span), F32), vecs=((8, D), F32), out_own_v=((L, D), F32), out_recv=((max(ny - 1, 1), L, D), BF),
         p_out=((nz, nx, B, E), BF), zr_out=((fz, nx, B, E), BF), xr_out=((fx, B, E), BF),

time: 176 us -> 164 us (0.932)
  Pallas kernels: 173 us -> 162 us
    pallas_call x2, Pallas kernels: 168 us -> 157 us  [call(): pl.pallas_call(functools.partial(kernel, s, names), name=name, out_shape=...]
where the time goes in v1:
time: 164 us
  Pallas kernels  162 us (99%)
    pallas_call x2, Pallas kernels, call(): pl.pallas_call(functools.partial(kernel, s, names), name=name, out_shape=...  157 us
    pallas_call x1, Pallas kernels, finish(): pl.pallas_call(functools.partial(finish_kernel, count), name='finish', ou...  4.9 us

profile of v1, /device:TPU:0, one launch (start us, length us, event | category | flops | bytes accessed | tf_op | source)
XLA Modules:
  0.0 164.1 jit_solution(3035342570251318390)
XLA Ops:
  0.6 71.0 %forward.1 = (f32[64,1536]{1,0:T(8,128)}, f32[64,1536]{1,0:T(8,128)}, f32[8,1536]{1,0:T(8,128)}, bf16[1280,1536]{1,0:T(8,128)(2,1)}, bf16[4,320,384]{2,1,0:T(8,1...) custom-call(bf16[256,1536]{1,0:T(8,128)(2,1)} %bitcast.19, ...), custom_call_target="tpu_custom_call" | custom-call | flops 8000000000 | bytes 40000000 | tf_op jit(solution)/shard_map/forward/pallas_call | solution.py:527
  71.6 86.2 %backward.1 = (f32[256,1536]{1,0:T(8,128)}, f32[64,1536]{1,0:T(8,128)}, f32[192,384]{1,0:T(8,128)}, f32[192,384]{1,0:T(8,128)}, f32[192,384]{1,0:T(8,128)}, /*in...) custom-call(bf16[256,1536]{1,0:T(8,128)(2,1)} %bitcast.20, ...), custom_call_target="tpu_custom_call" | custom-call | flops 30000001024 | bytes 80000000 | tf_op jit(solution)/shard_map/backward/pallas_call | solution.py:527
  157.8 4.9 %finish.1 = (f32[64,1536]{1,0:T(8,128)}, f32[256,1536]{1,0:T(8,128)}, f32[64,1536]{1,0:T(8,128)}, f32[192,384]{1,0:T(8,128)}, f32[192,384]{1,0:T(8,128)}, /*inde...) custom-call(f32[64,1536]{1,0:T(8,128)} %get-tuple-element.66.refs_0_, ...), custom_call_target="tpu_custom_call" | custom-call | tf_op jit(solution)/shard_map/finish/pallas_call | solution.py:952
  162.8 0.8 constant_dynamic-slice_fusion
  163.5 0.5 slice_bitcast_fusion
